TPU v7x, 32 devices: a whole 2x2x4 slice. The times are simulated.
32 devices in a mesh: grp: 2 (over x), ctx: 4 (over y, core), head: 4 (over z).
Axes of the slice: x: 2, y: 2, z: 4, core: 2. Of those that a mesh axis runs over, the one named last changes fastest.
Arguments:
- queries: bfloat16 [4096, 1024], P(('grp', 'ctx'), 'head'), parts along dimension 0, may hold values from -8 to 8
- keys: bfloat16 [4096, 1024], P(('grp', 'ctx'), 'head'), parts along dimension 0, may hold values from -8 to 8
- values: bfloat16 [4096, 1024], P(('grp', 'ctx'), 'head'), parts along dimension 0, may hold values from -6 to 6
- grad_out: bfloat16 [4096, 1024], P(('grp', 'ctx'), 'head'), parts along dimension 0, may hold values from -96 to 96
- block_docs: int32 [32], P('grp'), parts along dimension 0, may hold values from 0 to 7, never falling along the last dimension, each value on 1 to 6 neighbouring positions
- block_order: int32 [32], P('grp'), parts along dimension 0, may hold values from 0 to 15, as said below
Outputs:
- grad_queries: bfloat16 [4096, 1024], P(('grp', 'ctx'), 'head'), parts along dimension 0
- grad_keys: bfloat16 [4096, 1024], P(('grp', 'ctx'), 'head'), parts along dimension 0
- grad_values: bfloat16 [4096, 1024], P(('grp', 'ctx'), 'head'), parts along dimension 0
There are 2 independent parts, one for each index of `grp`. A program takes and returns all parts, laid end to end along the dimension named above; each array names one. Nothing has to cross between parts.
Inputs may be any that keep to these rules, and one draw needn't show every extreme that they name: `block_docs`: never falling along the pack; every shot covers 1 to 6 blocks, one exactly 6. `block_order`: every block exactly once; the 4 positions p with the same p // 4 take at most 1 blocks b with the same b // 4, and some such pair takes exactly 1.
All inputs are finite; a program needn't handle non-finite values.
Results may differ from a plain program's by a relative error of at most 0.0092.
Values may be sent and summed in bfloat16 or wider, within the bound.
No kernel may reach another device: no remote copies, remote signals or barrier semaphores. Data moves between devices by JAX's collectives and lax.ppermute only.
A program may use at most 64 MiB of HBM per device.

v0:
```python
import functools

import jax
import jax.numpy as jnp
import numpy as np
from jax import lax
from jax.experimental import pallas as pl
from jax.experimental.pallas import tpu as pltpu
from jax.sharding import PartitionSpec as P

HEAD_DIM = 128
BLOCK = 128
ARRAYS = 4
NEG_FILL = -1e30
SCALE = HEAD_DIM**-0.5
EXP2_SCALE = SCALE * float(np.log2(np.e))
NT = (((1,), (1,)), ((), ()))
TN = (((0,), (0,)), ((), ()))
NN = (((1,), (0,)), ((), ()))
ANY = pl.BlockSpec(memory_space=pl.ANY)
VMEM = pl.BlockSpec(memory_space=pltpu.VMEM)
SMEM = pl.BlockSpec(memory_space=pltpu.SMEM)


def dot(a, b, dims):
    return lax.dot_general(a, b, dims, preferred_element_type=jnp.float32)


def position_of(order, device, group):
    place = jnp.int32(0)
    block = jnp.int32(0)
    for j in range(4):
        candidate = order[device * 4 + j]
        hit = candidate // 4 == group
        place = jnp.where(hit, j, place)
        block = jnp.where(hit, candidate, block)
    return place, block


def slot_group(device, slot):
    return jnp.where(device // 2 == 0, (2, 3, 1, 0)[slot], (1, 0, 2, 3)[slot])


def pack_slots(heads, order, queries, keys, values, grad_out, *outs):
    me = lax.axis_index("ctx")
    for slot in range(4):
        place, _ = position_of(order, me, slot_group(me, slot))
        rows = pl.ds(pl.multiple_of(place * BLOCK, BLOCK), BLOCK)
        for array, source in enumerate((keys, values, queries, grad_out)):
            for head in range(heads):
                outs[head][slot, array] = source[rows, head * HEAD_DIM : (head + 1) * HEAD_DIM]


def one_doc(length, exact, start, end, base, blocks, held, prob, dsc, outs):
    window = start if exact else jnp.minimum(start, blocks - length)
    rows = length * BLOCK
    whole = pl.ds(pl.multiple_of(window * BLOCK, BLOCK), rows)
    keys = held[0, whole, :]
    values = held[1, whole, :]
    pair = min(2, length)
    if not exact:
        key_block = window + lax.broadcasted_iota(jnp.int32, (rows, pair * BLOCK), 0) // BLOCK
        key_ok = (key_block >= start) & (key_block < end)

    def stats(first):
        at = window + first
        these = pl.ds(pl.multiple_of(at * BLOCK, BLOCK), pair * BLOCK)
        queries = held[2, these, :]
        douts = held[3, these, :]
        scores = dot(keys, queries, NT) * EXP2_SCALE
        dprob = dot(values, douts, NT)
        if not exact:
            scores = jnp.where(key_ok, scores, NEG_FILL)
        top = jnp.max(scores, axis=0, keepdims=True)
        weights = jnp.exp2(scores - top)
        inverse = 1.0 / jnp.sum(weights, axis=0, keepdims=True)
        probabilities = weights * inverse
        delta = jnp.sum(probabilities * dprob, axis=0, keepdims=True)
        dscore = probabilities * (dprob - delta)
        if not exact:
            query_block = at + lax.broadcasted_iota(jnp.int32, (rows, pair * BLOCK), 1) // BLOCK
            ok = key_ok & (query_block >= start) & (query_block < end)
            probabilities = jnp.where(ok, probabilities, 0.0)
            dscore = jnp.where(ok, dscore, 0.0)
        return probabilities.astype(jnp.bfloat16), dscore.astype(jnp.bfloat16)

    queries = held[2, whole, :]
    douts = held[3, whole, :]

    def store(block, prob_rows, dsc_rows, dsc_columns):
        query_grad, key_grad, value_grad = outs
        to = pl.ds(pl.multiple_of((block - base) * BLOCK, BLOCK), BLOCK)
        value_grad[to, :] = dot(prob_rows, douts, NN).astype(jnp.bfloat16)
        key_grad[to, :] = (dot(dsc_rows, queries, NN) * SCALE).astype(jnp.bfloat16)
        query_grad[to, :] = (dot(dsc_columns, keys, TN) * SCALE).astype(jnp.bfloat16)

    if exact and length <= 2:
        prob_low, dsc_low = stats(0)
        for i in range(length):
            mine = slice(i * BLOCK, (i + 1) * BLOCK)
            block = start + i
            pl.when((block >= base) & (block < base + 4))(
                functools.partial(store, block, prob_low[mine], dsc_low[mine], dsc_low[:, mine])
            )
        return

    def columns_of(step, carry):
        first = jnp.minimum(step * pair, length - pair)
        columns = pl.ds(pl.multiple_of(first * BLOCK, BLOCK), pair * BLOCK)
        prob[0:rows, columns], dsc[0:rows, columns] = stats(first)
        return carry

    def block_of(block, carry):
        mine = pl.ds(pl.multiple_of((block - window) * BLOCK, BLOCK), BLOCK)
        store(block, prob[mine, 0:rows], dsc[mine, 0:rows], dsc[0:rows, mine])
        return carry

    lax.fori_loop(0, -(-length // pair), columns_of, 0)
    lax.fori_loop(jnp.maximum(start, base), jnp.minimum(end, base + 4), block_of, 0)


def all_docs(blocks, longest, base, docs, held, prob, dsc, outs):
    if longest <= 8:
        sizes = list(range(1, longest + 1))
    else:
        step = -(-longest // 6)
        sizes = [min(longest, step * (i + 1)) for i in range(-(-longest // step))]

    def visit(t, carry):
        block = base + t
        doc = docs[block]
        begins = jnp.logical_or(t == 0, docs[jnp.maximum(block - 1, 0)] != doc)

        @pl.when(begins)
        def _():
            start = lax.fori_loop(0, blocks, lambda b, c: c + (docs[b] < doc).astype(jnp.int32), 0)
            end = lax.fori_loop(0, blocks, lambda b, c: c + (docs[b] <= doc).astype(jnp.int32), 0)
            length = end - start
            below = 0
            for size in sizes:
                pl.when((length > below) & (length <= size))(
                    functools.partial(
                        one_doc, size, size - below == 1, start, end, base, blocks, held, prob, dsc, outs
                    )
                )
                below = size

        return carry

    lax.fori_loop(0, 4, visit, 0)


def attend_slots(blocks, longest, order, docs, own, core, row, diag, *rest):
    outs, (held, prob, dsc, sems) = rest[-7:-4], rest[-4:]
    me = lax.axis_index("ctx")
    copies = []
    for flip, source in ((0, own), (1, core), (2, row), (3, diag)):
        device = me ^ flip
        for slot in range(source.shape[0]):
            _, block = position_of(order, device, slot_group(device, slot))
            to = pl.ds(pl.multiple_of(block * BLOCK, BLOCK), BLOCK)
            copies.append(
                pltpu.make_async_copy(source.at[slot], held.at[:, to, :], sems.at[len(copies)])
            )
    for copy in copies:
        copy.start()
    for copy in copies:
        copy.wait()
    all_docs(blocks, longest, me * 4, docs, held, prob, dsc, outs)


def attend_gathered(blocks, longest, head, order, docs, queries, keys, values, grad_out, *rest):
    outs, (held, prob, dsc, sems) = rest[-7:-4], rest[-4:]
    me = lax.axis_index("ctx")

    def copies(position):
        rows = pl.ds(pl.multiple_of(position * BLOCK, BLOCK), BLOCK)
        to = pl.ds(pl.multiple_of(order[position] * BLOCK, BLOCK), BLOCK)
        return [
            pltpu.make_async_copy(
                source.at[rows, pl.ds(head * HEAD_DIM, HEAD_DIM)],
                held.at[array, to, :],
                sems.at[position * ARRAYS + array],
            )
            for array, source in enumerate((keys, values, queries, grad_out))
        ]

    def begin(position, carry):
        for copy in copies(position):
            copy.start()
        return carry

    def finish(position, carry):
        for copy in copies(position):
            copy.wait()
        return carry

    lax.fori_loop(0, blocks, begin, 0)
    lax.fori_loop(0, blocks, finish, 0)
    all_docs(blocks, longest, me * 4, docs, held, prob, dsc, outs)


def attend(kernel, head, sources, previous, order, docs, rows, heads, blocks, longest):
    out = jax.ShapeDtypeStruct((rows, heads * HEAD_DIM), jnp.bfloat16)
    first = 2 + len(sources)
    return pl.pallas_call(
        kernel,
        out_shape=(out,) * 3,
        grid=(1,),
        in_specs=[SMEM, SMEM] + [ANY] * (len(sources) + len(previous)),
        out_specs=[pl.BlockSpec((rows, HEAD_DIM), lambda i: (0, head))] * 3,
        scratch_shapes=[
            pltpu.VMEM((ARRAYS, blocks * BLOCK, HEAD_DIM), jnp.bfloat16),
            pltpu.VMEM((longest * BLOCK, longest * BLOCK), jnp.bfloat16),
            pltpu.VMEM((longest * BLOCK, longest * BLOCK), jnp.bfloat16),
            pltpu.SemaphoreType.DMA((blocks * ARRAYS,)),
        ],
        input_output_aliases={first + i: i for i in range(len(previous))},
        compiler_params=pltpu.CompilerParams(vmem_limit_bytes=60 << 20),
        cost_estimate=pl.CostEstimate(
            flops=300 * 2 * 128**3, bytes_accessed=4 << 20, transcendentals=60 * 128 * 128
        ),
        name="attend",
    )(order, docs, *sources, *previous)


def local(queries, keys, values, grad_out, block_docs, block_order):
    rows, width = queries.shape
    heads = width // HEAD_DIM
    blocks = block_order.shape[0]
    devices = lax.axis_size("ctx")
    longest = blocks * 3 // 8
    grads = ()
    if devices != 4:
        gathered = [
            lax.all_gather(x, "ctx", axis=0, tiled=True) for x in (queries, keys, values, grad_out)
        ]
        for head in range(heads):
            kernel = functools.partial(attend_gathered, blocks, longest, head)
            grads = attend(
                kernel, head, gathered, grads, block_order, block_docs, rows, heads, blocks, longest
            )
        return grads

    def swap(array, flip):
        return lax.ppermute(array, "ctx", [(i, i ^ flip) for i in range(4)])

    slots = jax.ShapeDtypeStruct((4, ARRAYS, BLOCK, HEAD_DIM), jnp.bfloat16)
    own = pl.pallas_call(
        functools.partial(pack_slots, heads),
        out_shape=(slots,) * heads,
        in_specs=[SMEM] + [VMEM] * ARRAYS,
        out_specs=(VMEM,) * heads,
        compiler_params=pltpu.CompilerParams(vmem_limit_bytes=16 << 20),
        name="pack",
    )(block_order, queries, keys, values, grad_out)
    row = [swap(x, 2) for x in own]
    core = [swap(x, 1) for x in own]
    diag = [swap(x, 1) for x in row]
    for head in range(heads):
        kernel = functools.partial(attend_slots, blocks, longest)
        sources = (own[head], core[head], row[head], diag[head])
        grads = attend(
            kernel, head, sources, grads, block_order, block_docs, rows, heads, blocks, longest
        )
    return grads


def solution(mesh):
    rows = P(("grp", "ctx"), "head")
    return jax.shard_map(
        local,
        mesh=mesh,
        in_specs=(rows, rows, rows, rows, P("grp"), P("grp")),
        out_specs=(rows, rows, rows),
        check_vma=False,
    )
```

profile of v0, /device:TPU:1, one launch (start us, length us, event | category | flops | bytes accessed | tf_op | source)
XLA Modules:
  0.0 49.4 jit_solution(14753686582314315543)
XLA Ops:
  0.6 0.0 copy-start
  0.6 0.9 %copy-done = bf16[512,256]{1,0:T(8,128)(2,1)S(1)} copy-done((bf16[512,256]{1,0:T(8,128)(2,1)S(1)}, bf16[512,256]{1,0:T(8,128)(2,1)}, u32[]{:S(2)}) %copy-start) | copy-done | bytes 262168
  1.6 0.0 copy-start.1
  1.6 0.9 %copy-done.1 = bf16[512,256]{1,0:T(8,128)(2,1)S(1)} copy-done((bf16[512,256]{1,0:T(8,128)(2,1)S(1)}, bf16[512,256]{1,0:T(8,128)(2,1)}, u32[]{:S(2)}) %copy-start.1) | copy-done | bytes 262168
  2.5 0.0 copy-start.2
  2.5 0.9 %copy-done.2 = bf16[512,256]{1,0:T(8,128)(2,1)S(1)} copy-done((bf16[512,256]{1,0:T(8,128)(2,1)S(1)}, bf16[512,256]{1,0:T(8,128)(2,1)}, u32[]{:S(2)}) %copy-start.2) | copy-done | bytes 262168
  3.5 0.0 copy-start.3
  3.5 0.9 %copy-done.3 = bf16[512,256]{1,0:T(8,128)(2,1)S(1)} copy-done((bf16[512,256]{1,0:T(8,128)(2,1)S(1)}, bf16[512,256]{1,0:T(8,128)(2,1)}, u32[]{:S(2)}) %copy-start.3) | copy-done | bytes 262168
  4.4 0.0 copy-start.4
  4.4 0.7 %copy-done.4 = s32[16]{0:T(128)S(1)} copy-done((s32[16]{0:T(128)S(1)}, s32[16]{0:T(128)}, u32[]{:S(2)}) %copy-start.4) | copy-done | bytes 88
  5.1 0.8 %pack.1 = (bf16[4,4,128,128]{3,2,1,0:T(8,128)(2,1)S(1)}, bf16[4,4,128,128]{3,2,1,0:T(8,128)(2,1)S(1)}) custom-call(s32[16]{0:T(128)S(1)} %copy-done.4, bf16[512,256]{1,0:T(8,128)(2,1)S(1)} %copy-done, bf16[512,256]{1,0:T(8,128)(2,1)S(1)} %copy-done.1, bf16[512,256]{1,0:T(8,128)(2,1)S(1)} %copy-done.2, bf16[512,256]{1,0:T(8,128)(2,1)S(1)} %copy-done.3), custom_call_target="tpu_custom_call" | custom-call | tf_op jit(solution)/shard_map/pack/pallas_call | solution.py:249
  5.9 0.0 copy-start.6
  5.9 0.0 copy-start.5
  5.9 2.1 %collective-permute-start.4 = (bf16[4,4,128,128]{3,2,1,0:T(8,128)(2,1)S(1)}, bf16[4,4,128,128]{3,2,1,0:T(8,128)(2,1)S(1)}, u32[]{:S(2)}, u32[]{:S(2)}) collective-permute-start(bf16[4,4,128,128]{3,2,1,0:T(8,128)(2,1)S(1)} %get-tuple-element.9.own), channel_id=1, source_target_pairs={{0,8},{4,12},{8,0},{12,4},{1,9},{5,13},{9,1},{13,5},{2,10},{6,14},... | collective-permute-start | bytes 1572872 | tf_op jit(solution)/shard_map/ppermute | solution.py:246
  8.1 0.1 collective-permute-start.1
  8.1 1.0 %collective-permute-start.3 = (bf16[4,4,128,128]{3,2,1,0:T(8,128)(2,1)S(1)}, bf16[4,4,128,128]{3,2,1,0:T(8,128)(2,1)S(1)}, u32[]{:S(2)}, u32[]{:S(2)}) collective-permute-start(bf16[4,4,128,128]{3,2,1,0:T(8,128)(2,1)S(1)} %get-tuple-element.9.own), channel_id=1, source_target_pairs={{0,4},{4,0},{8,12},{12,8},{1,5},{5,1},{9,13},{13,9},{2,6},{6,2},{1... | collective-permute-start | bytes 1572872 | tf_op jit(solution)/shard_map/ppermute | solution.py:246
  9.1 10.6 %collective-permute-done.4.row = bf16[4,4,128,128]{3,2,1,0:T(8,128)(2,1)S(1)} collective-permute-done((bf16[4,4,128,128]{3,2,1,0:T(8,128)(2,1)S(1)}, bf16[4,4,128,128]{3,2,1,0:T(8,128)(2,1)S(1)}, u32[]{:S(2)}, u32[]{:S(2)}) %collective-permute-start.4) | collective-permute-done | bytes 524320 | tf_op jit(solution)/shard_map/ppermute | solution.py:246
  19.7 0.0 copy-start.8
  19.7 2.1 %collective-permute-start.5 = (bf16[4,4,128,128]{3,2,1,0:T(8,128)(2,1)S(1)}, bf16[4,4,128,128]{3,2,1,0:T(8,128)(2,1)}, u32[]{:S(2)}, u32[]{:S(2)}) collective-permute-start(bf16[4,4,128,128]{3,2,1,0:T(8,128)(2,1)S(1)} %collective-permute-done.4.row), channel_id=1, source_target_pairs={{0,4},{4,0},{8,12},{12,8},{1,5},{5,1},{9,13},{13,9},{2,6},{6,2},{1... | collective-permute-start | bytes 1572872 | tf_op jit(solution)/shard_map/ppermute | solution.py:246
  21.8 0.0 collective-permute-start
  21.8 9.2 %collective-permute-done.1.row = bf16[4,4,128,128]{3,2,1,0:T(8,128)(2,1)S(1)} collective-permute-done((bf16[4,4,128,128]{3,2,1,0:T(8,128)(2,1)S(1)}, bf16[4,4,128,128]{3,2,1,0:T(8,128)(2,1)S(1)}, u32[]{:S(2)}, u32[]{:S(2)}) %collective-permute-start.1) | collective-permute-done | bytes 524320 | tf_op jit(solution)/shard_map/ppermute | solution.py:246
  30.9 0.0 copy-start.7
  30.9 1.2 %collective-permute-start.2 = (bf16[4,4,128,128]{3,2,1,0:T(8,128)(2,1)S(1)}, bf16[4,4,128,128]{3,2,1,0:T(8,128)(2,1)S(1)}, u32[]{:S(2)}, u32[]{:S(2)}) collective-permute-start(bf16[4,4,128,128]{3,2,1,0:T(8,128)(2,1)S(1)} %collective-permute-done.1.row), channel_id=1, source_target_pairs={{0,4},{4,0},{8,12},{12,8},{1,5},{5,1},{9,13},{13,9},{2,6},{6,2},{1... | collective-permute-start | bytes 1572872 | tf_op jit(solution)/shard_map/ppermute | solution.py:246
  32.2 0.0 collective-permute-done.3.core
  32.2 0.0 copy-start.10
  32.2 0.0 collective-permute-done.5.diag
  32.2 0.0 copy-done.6
  32.2 0.0 copy-done.8
  32.2 0.8 %copy-done.10 = bf16[4,4,128,128]{3,2,1,0:T(8,128)(2,1)} copy-done((bf16[4,4,128,128]{3,2,1,0:T(8,128)(2,1)}, bf16[4,4,128,128]{3,2,1,0:T(8,128)(2,1)S(1)}, u32[]{:S(2)}) %copy-start.10) | copy-done | bytes 524312
  33.0 7.7 %attend.2 = (bf16[512,256]{1,0:T(8,128)(2,1)}, bf16[512,256]{1,0:T(8,128)(2,1)}, bf16[512,256]{1,0:T(8,128)(2,1)}) custom-call(s32[16]{0:T(128)} %order.5, s32[16]{0:T(128)} %docs.3, bf16[4,4,128,128]{3,2,1,0:T(8,128)(2,1)} %copy-done.6, bf16[4,4,128,128]{3,2,1,0:T(8,128)(2,1)} %copy-done.10, bf16[4,4,128,128]{3,2,1,0:T(8,128)(2,1)} %copy-done.8, ...), custom_call_target="tpu_custom_call" | custom-call | flops 1258291200 | bytes 4194304 | tf_op jit(solution)/shard_map/attend/pallas_call | solution.py:206
  40.7 0.0 copy-done.5
  40.7 0.0 copy-done.7
  40.7 0.0 collective-permute-done.core
  40.7 0.0 copy-start.9
  40.7 0.0 collective-permute-done.2.diag
  40.7 0.0 copy-start.11
  40.7 0.8 %copy-done.9 = bf16[4,4,128,128]{3,2,1,0:T(8,128)(2,1)} copy-done((bf16[4,4,128,128]{3,2,1,0:T(8,128)(2,1)}, bf16[4,4,128,128]{3,2,1,0:T(8,128)(2,1)S(1)}, u32[]{:S(2)}) %copy-start.9) | copy-done | bytes 524312
  41.5 0.2 copy-done.11
  41.7 7.7 %attend.3 = (bf16[512,256]{1,0:T(8,128)(2,1)}, bf16[512,256]{1,0:T(8,128)(2,1)}, bf16[512,256]{1,0:T(8,128)(2,1)}) custom-call(s32[16]{0:T(128)} %order.5, s32[16]{0:T(128)} %docs.3, bf16[4,4,128,128]{3,2,1,0:T(8,128)(2,1)} %copy-done.5, bf16[4,4,128,128]{3,2,1,0:T(8,128)(2,1)} %copy-done.9, ...), custom_call_target="tpu_custom_call", output_to_operand_aliasing={{0}: (6, {}), {1}: (7, {}), {2}: (8, {})} | custom-call | flops 1258291200 | bytes 4194304 | tf_op jit(solution)/shard_map/attend/pallas_call | solution.py:206
Async XLA Ops:
  0.6 1.0 %copy-start = (bf16[512,256]{1,0:T(8,128)(2,1)S(1)}, bf16[512,256]{1,0:T(8,128)(2,1)}, u32[]{:S(2)}) copy-start(bf16[512,256]{1,0:T(8,128)(2,1)} %queries.1) | copy-start | bytes 786436
  1.6 0.9 %copy-start.1 = (bf16[512,256]{1,0:T(8,128)(2,1)S(1)}, bf16[512,256]{1,0:T(8,128)(2,1)}, u32[]{:S(2)}) copy-start(bf16[512,256]{1,0:T(8,128)(2,1)} %keys.1) | copy-start | bytes 786436
  2.5 0.9 %copy-start.2 = (bf16[512,256]{1,0:T(8,128)(2,1)S(1)}, bf16[512,256]{1,0:T(8,128)(2,1)}, u32[]{:S(2)}) copy-start(bf16[512,256]{1,0:T(8,128)(2,1)} %values.1) | copy-start | bytes 786436
  3.5 0.9 %copy-start.3 = (bf16[512,256]{1,0:T(8,128)(2,1)S(1)}, bf16[512,256]{1,0:T(8,128)(2,1)}, u32[]{:S(2)}) copy-start(bf16[512,256]{1,0:T(8,128)(2,1)} %grad_out.1) | copy-start | bytes 786436
  4.4 0.7 %copy-start.4 = (s32[16]{0:T(128)S(1)}, s32[16]{0:T(128)}, u32[]{:S(2)}) copy-start(s32[16]{0:T(128)} %order.5) | copy-start | bytes 196
  5.9 26.3 %copy-start.6 = (bf16[4,4,128,128]{3,2,1,0:T(8,128)(2,1)}, bf16[4,4,128,128]{3,2,1,0:T(8,128)(2,1)S(1)}, u32[]{:S(2)}) copy-start(bf16[4,4,128,128]{3,2,1,0:T(8,128)(2,1)S(1)} %get-tuple-element.9.own) | copy-start | bytes 1572868
  5.9 34.8 %copy-start.5 = (bf16[4,4,128,128]{3,2,1,0:T(8,128)(2,1)}, bf16[4,4,128,128]{3,2,1,0:T(8,128)(2,1)S(1)}, u32[]{:S(2)}) copy-start(bf16[4,4,128,128]{3,2,1,0:T(8,128)(2,1)S(1)} %get-tuple-element.8.own) | copy-start | bytes 1572868
  5.9 13.8 %collective-permute-start.4 = (bf16[4,4,128,128]{3,2,1,0:T(8,128)(2,1)S(1)}, bf16[4,4,128,128]{3,2,1,0:T(8,128)(2,1)S(1)}, u32[]{:S(2)}, u32[]{:S(2)}) collective-permute-start(bf16[4,4,128,128]{3,2,1,0:T(8,128)(2,1)S(1)} %get-tuple-element.9.own), channel_id=1, source_target_pairs={{0,8},{4,12},{8,0},{12,4},{1,9},{5,13},{9,1},{13,5},{2,10},{6,14},... | collective-permute-start | bytes 1572872 | tf_op jit(solution)/shard_map/ppermute | solution.py:246
  8.1 22.9 %collective-permute-start.1 = (bf16[4,4,128,128]{3,2,1,0:T(8,128)(2,1)S(1)}, bf16[4,4,128,128]{3,2,1,0:T(8,128)(2,1)S(1)}, u32[]{:S(2)}, u32[]{:S(2)}) collective-permute-start(bf16[4,4,128,128]{3,2,1,0:T(8,128)(2,1)S(1)} %get-tuple-element.8.own), channel_id=1, source_target_pairs={{0,8},{4,12},{8,0},{12,4},{1,9},{5,13},{9,1},{13,5},{2,10},{6,14},... | collective-permute-start | bytes 1572872 | tf_op jit(solution)/shard_map/ppermute | solution.py:246
  8.1 24.0 %collective-permute-start.3 = (bf16[4,4,128,128]{3,2,1,0:T(8,128)(2,1)S(1)}, bf16[4,4,128,128]{3,2,1,0:T(8,128)(2,1)S(1)}, u32[]{:S(2)}, u32[]{:S(2)}) collective-permute-start(bf16[4,4,128,128]{3,2,1,0:T(8,128)(2,1)S(1)} %get-tuple-element.9.own), channel_id=1, source_target_pairs={{0,4},{4,0},{8,12},{12,8},{1,5},{5,1},{9,13},{13,9},{2,6},{6,2},{1... | collective-permute-start | bytes 1572872 | tf_op jit(solution)/shard_map/ppermute | solution.py:246
  19.7 12.5 %copy-start.8 = (bf16[4,4,128,128]{3,2,1,0:T(8,128)(2,1)}, bf16[4,4,128,128]{3,2,1,0:T(8,128)(2,1)S(1)}, u32[]{:S(2)}) copy-start(bf16[4,4,128,128]{3,2,1,0:T(8,128)(2,1)S(1)} %collective-permute-done.4.row) | copy-start | bytes 1572868
  19.7 12.5 %collective-permute-start.5 = (bf16[4,4,128,128]{3,2,1,0:T(8,128)(2,1)S(1)}, bf16[4,4,128,128]{3,2,1,0:T(8,128)(2,1)}, u32[]{:S(2)}, u32[]{:S(2)}) collective-permute-start(bf16[4,4,128,128]{3,2,1,0:T(8,128)(2,1)S(1)} %collective-permute-done.4.row), channel_id=1, source_target_pairs={{0,4},{4,0},{8,12},{12,8},{1,5},{5,1},{9,13},{13,9},{2,6},{6,2},{1... | collective-permute-start | bytes 1572872 | tf_op jit(solution)/shard_map/ppermute | solution.py:246
  21.8 18.9 %collective-permute-start = (bf16[4,4,128,128]{3,2,1,0:T(8,128)(2,1)S(1)}, bf16[4,4,128,128]{3,2,1,0:T(8,128)(2,1)S(1)}, u32[]{:S(2)}, u32[]{:S(2)}) collective-permute-start(bf16[4,4,128,128]{3,2,1,0:T(8,128)(2,1)S(1)} %get-tuple-element.8.own), channel_id=1, source_target_pairs={{0,4},{4,0},{8,12},{12,8},{1,5},{5,1},{9,13},{13,9},{2,6},{6,2},{1... | collective-permute-start | bytes 1572872 | tf_op jit(solution)/shard_map/ppermute | solution.py:246
  30.9 9.7 %copy-start.7 = (bf16[4,4,128,128]{3,2,1,0:T(8,128)(2,1)}, bf16[4,4,128,128]{3,2,1,0:T(8,128)(2,1)S(1)}, u32[]{:S(2)}) copy-start(bf16[4,4,128,128]{3,2,1,0:T(8,128)(2,1)S(1)} %collective-permute-done.1.row) | copy-start | bytes 1572868
  30.9 9.8 %collective-permute-start.2 = (bf16[4,4,128,128]{3,2,1,0:T(8,128)(2,1)S(1)}, bf16[4,4,128,128]{3,2,1,0:T(8,128)(2,1)S(1)}, u32[]{:S(2)}, u32[]{:S(2)}) collective-permute-start(bf16[4,4,128,128]{3,2,1,0:T(8,128)(2,1)S(1)} %collective-permute-done.1.row), channel_id=1, source_target_pairs={{0,4},{4,0},{8,12},{12,8},{1,5},{5,1},{9,13},{13,9},{2,6},{6,2},{1... | collective-permute-start | bytes 1572872 | tf_op jit(solution)/shard_map/ppermute | solution.py:246
  32.2 0.8 %copy-start.10 = (bf16[4,4,128,128]{3,2,1,0:T(8,128)(2,1)}, bf16[4,4,128,128]{3,2,1,0:T(8,128)(2,1)S(1)}, u32[]{:S(2)}) copy-start(bf16[4,4,128,128]{3,2,1,0:T(8,128)(2,1)S(1)} %collective-permute-done.3.core) | copy-start | bytes 1572868
  40.7 0.8 %copy-start.9 = (bf16[4,4,128,128]{3,2,1,0:T(8,128)(2,1)}, bf16[4,4,128,128]{3,2,1,0:T(8,128)(2,1)S(1)}, u32[]{:S(2)}) copy-start(bf16[4,4,128,128]{3,2,1,0:T(8,128)(2,1)S(1)} %collective-permute-done.core) | copy-start | bytes 1572868
  40.7 1.0 %copy-start.11 = (bf16[4,4,128,128]{3,2,1,0:T(8,128)(2,1)}, bf16[4,4,128,128]{3,2,1,0:T(8,128)(2,1)S(1)}, u32[]{:S(2)}) copy-start(bf16[4,4,128,128]{3,2,1,0:T(8,128)(2,1)S(1)} %collective-permute-done.2.diag) | copy-start | bytes 1572868
where the time goes:
time: 49.7 us; the launch traced here: 49.4 us
  waiting for transfers between devices  19.8 us (40%)
  Pallas kernels  16.2 us (33%)
  starting transfers between devices  6.46 us (13%)
  local copies, waits for them, and re-layouts  6.19 us (12%)
  between operations  0.75 us (2%)
    ppermute x6, waiting for transfers between devices, swap(): return lax.ppermute(array, 'ctx', [(i, i ^ flip) for i in range(4)])  19.8 us
    pallas_call x2, Pallas kernels, attend(): pl.pallas_call(kernel, out_shape=(out,) * 3, grid=(1,), in_specs=[SMEM, S...  15.4 us
    ppermute x6, starting transfers between devices, swap(): return lax.ppermute(array, 'ctx', [(i, i ^ flip) for i in range(4)])  6.46 us
    unnamed x24, local copies, waits for them, and re-layouts  6.19 us
  transfers between devices with their start and end apart: 6, of which 2 were waited for; matrix products, arithmetic and copies ran while one was open for 0% of the time, Pallas kernels for 16%

commit v1 on v0

--- a/solution.py
+++ b/solution.py
@@ -19,6 +19,7 @@
 NN = (((1,), (0,)), ((), ()))
 ANY = pl.BlockSpec(memory_space=pl.ANY)
 VMEM = pl.BlockSpec(memory_space=pltpu.VMEM)
+HBM = pl.BlockSpec(memory_space=pltpu.HBM)
 SMEM = pl.BlockSpec(memory_space=pltpu.SMEM)
 
 
@@ -41,17 +42,27 @@
     return jnp.where(device // 2 == 0, (2, 3, 1, 0)[slot], (1, 0, 2, 3)[slot])
 
 
-def pack_slots(heads, order, queries, keys, values, grad_out, *outs):
+def pack_slots(heads, order_in, *rest):
+    sources, outs = rest[:ARRAYS], rest[ARRAYS : ARRAYS + heads]
+    order, staged, sems = rest[-3:]
     me = lax.axis_index("ctx")
+    copies = [pltpu.make_async_copy(order_in, order, sems.at[ARRAYS])]
+    for array, source in enumerate(sources):
+        copies.append(pltpu.make_async_copy(source, staged.at[array], sems.at[array]))
+    for copy in copies:
+        copy.start()
+    for copy in copies:
+        copy.wait()
     for slot in range(4):
         place, _ = position_of(order, me, slot_group(me, slot))
         rows = pl.ds(pl.multiple_of(place * BLOCK, BLOCK), BLOCK)
-        for array, source in enumerate((keys, values, queries, grad_out)):
+        for array in range(ARRAYS):
             for head in range(heads):
-                outs[head][slot, array] = source[rows, head * HEAD_DIM : (head + 1) * HEAD_DIM]
-
-
-def one_doc(length, exact, start, end, base, blocks, held, prob, dsc, outs):
+                columns = slice(head * HEAD_DIM, (head + 1) * HEAD_DIM)
+                outs[head][slot, array] = staged[array, rows, columns]
+
+
+def one_doc(length, exact, start, end, base, blocks, held, prob, dsc, results):
     window = start if exact else jnp.minimum(start, blocks - length)
     rows = length * BLOCK
     whole = pl.ds(pl.multiple_of(window * BLOCK, BLOCK), rows)
@@ -88,11 +99,13 @@
     douts = held[3, whole, :]
 
     def store(block, prob_rows, dsc_rows, dsc_columns):
-        query_grad, key_grad, value_grad = outs
-        to = pl.ds(pl.multiple_of((block - base) * BLOCK, BLOCK), BLOCK)
-        value_grad[to, :] = dot(prob_rows, douts, NN).astype(jnp.bfloat16)
-        key_grad[to, :] = (dot(dsc_rows, queries, NN) * SCALE).astype(jnp.bfloat16)
-        query_grad[to, :] = (dot(dsc_columns, keys, TN) * SCALE).astype(jnp.bfloat16)
+        at = block - base
+        results.stage[2, at] = dot(prob_rows, douts, NN).astype(jnp.bfloat16)
+        results.copy(at, 2).start()
+        results.stage[1, at] = (dot(dsc_rows, queries, NN) * SCALE).astype(jnp.bfloat16)
+        results.copy(at, 1).start()
+        results.stage[0, at] = (dot(dsc_columns, keys, TN) * SCALE).astype(jnp.bfloat16)
+        results.copy(at, 0).start()
 
     if exact and length <= 2:
         prob_low, dsc_low = stats(0)
@@ -119,7 +132,19 @@
     lax.fori_loop(jnp.maximum(start, base), jnp.minimum(end, base + 4), block_of, 0)
 
 
-def all_docs(blocks, longest, base, docs, held, prob, dsc, outs):
+class Results:
+    def __init__(self, head, outs, stage, sems):
+        self.head, self.outs, self.stage, self.sems = head, outs, stage, sems
+
+    def copy(self, at, array):
+        rows = pl.ds(pl.multiple_of(at * BLOCK, BLOCK), BLOCK)
+        columns = pl.ds(self.head * HEAD_DIM, HEAD_DIM)
+        return pltpu.make_async_copy(
+            self.stage.at[array, at], self.outs[array].at[rows, columns], self.sems.at[at * 3 + array]
+        )
+
+
+def all_docs(blocks, longest, base, docs, held, prob, dsc, results):
     if longest <= 8:
         sizes = list(range(1, longest + 1))
     else:
@@ -133,14 +158,17 @@
 
         @pl.when(begins)
         def _():
-            start = lax.fori_loop(0, blocks, lambda b, c: c + (docs[b] < doc).astype(jnp.int32), 0)
-            end = lax.fori_loop(0, blocks, lambda b, c: c + (docs[b] <= doc).astype(jnp.int32), 0)
+            start, end = jnp.int32(0), jnp.int32(0)
+            for b in range(blocks):
+                other = docs[b]
+                start += (other < doc).astype(jnp.int32)
+                end += (other <= doc).astype(jnp.int32)
             length = end - start
             below = 0
             for size in sizes:
                 pl.when((length > below) & (length <= size))(
                     functools.partial(
-                        one_doc, size, size - below == 1, start, end, base, blocks, held, prob, dsc, outs
+                        one_doc, size, size - below == 1, start, end, base, blocks, held, prob, dsc, results
                     )
                 )
                 below = size
@@ -148,29 +176,30 @@
         return carry
 
     lax.fori_loop(0, 4, visit, 0)
-
-
-def attend_slots(blocks, longest, order, docs, own, core, row, diag, *rest):
-    outs, (held, prob, dsc, sems) = rest[-7:-4], rest[-4:]
+    for at in range(4):
+        for array in range(3):
+            results.copy(at, array).wait()
+
+
+def attend_slots(blocks, longest, head, places, order, docs, *rest):
+    outs, (held, prob, dsc, stage, sems) = rest[-8:-5], rest[-5:]
     me = lax.axis_index("ctx")
-    copies = []
-    for flip, source in ((0, own), (1, core), (2, row), (3, diag)):
+    low, high = docs[me * 4], docs[me * 4 + 3]
+    for (flip, first), source in zip(places, rest):
         device = me ^ flip
         for slot in range(source.shape[0]):
-            _, block = position_of(order, device, slot_group(device, slot))
-            to = pl.ds(pl.multiple_of(block * BLOCK, BLOCK), BLOCK)
-            copies.append(
-                pltpu.make_async_copy(source.at[slot], held.at[:, to, :], sems.at[len(copies)])
-            )
-    for copy in copies:
-        copy.start()
-    for copy in copies:
-        copy.wait()
-    all_docs(blocks, longest, me * 4, docs, held, prob, dsc, outs)
-
-
-def attend_gathered(blocks, longest, head, order, docs, queries, keys, values, grad_out, *rest):
-    outs, (held, prob, dsc, sems) = rest[-7:-4], rest[-4:]
+            _, block = position_of(order, device, slot_group(device, first + slot))
+
+            @pl.when((docs[block] >= low) & (docs[block] <= high))
+            def _(source=source, slot=slot, block=block):
+                to = pl.ds(pl.multiple_of(block * BLOCK, BLOCK), BLOCK)
+                held[:, to, :] = source[slot]
+
+    all_docs(blocks, longest, me * 4, docs, held, prob, dsc, Results(head, outs, stage, sems))
+
+
+def attend_gathered(blocks, longest, head, order, docs, keys, values, queries, grad_out, *rest):
+    outs, (held, prob, dsc, stage, out_sems, sems) = rest[-9:-6], rest[-6:]
     me = lax.axis_index("ctx")
 
     def copies(position):
@@ -197,28 +226,31 @@
 
     lax.fori_loop(0, blocks, begin, 0)
     lax.fori_loop(0, blocks, finish, 0)
-    all_docs(blocks, longest, me * 4, docs, held, prob, dsc, outs)
-
-
-def attend(kernel, head, sources, previous, order, docs, rows, heads, blocks, longest):
+    all_docs(blocks, longest, me * 4, docs, held, prob, dsc, Results(head, outs, stage, out_sems))
+
+
+def attend(kernel, sources, previous, order, docs, rows, blocks, longest, heads, gathered):
     out = jax.ShapeDtypeStruct((rows, heads * HEAD_DIM), jnp.bfloat16)
     first = 2 + len(sources)
+    scratch = [
+        pltpu.VMEM((ARRAYS, blocks * BLOCK, HEAD_DIM), jnp.bfloat16),
+        pltpu.VMEM((longest * BLOCK, longest * BLOCK), jnp.bfloat16),
+        pltpu.VMEM((longest * BLOCK, longest * BLOCK), jnp.bfloat16),
+        pltpu.VMEM((3, 4, BLOCK, HEAD_DIM), jnp.bfloat16),
+        pltpu.SemaphoreType.DMA((12,)),
+    ]
+    if gathered:
+        scratch.append(pltpu.SemaphoreType.DMA((blocks * ARRAYS,)))
     return pl.pallas_call(
         kernel,
         out_shape=(out,) * 3,
-        grid=(1,),
-        in_specs=[SMEM, SMEM] + [ANY] * (len(sources) + len(previous)),
-        out_specs=[pl.BlockSpec((rows, HEAD_DIM), lambda i: (0, head))] * 3,
-        scratch_shapes=[
-            pltpu.VMEM((ARRAYS, blocks * BLOCK, HEAD_DIM), jnp.bfloat16),
-            pltpu.VMEM((longest * BLOCK, longest * BLOCK), jnp.bfloat16),
-            pltpu.VMEM((longest * BLOCK, longest * BLOCK), jnp.bfloat16),
-            pltpu.SemaphoreType.DMA((blocks * ARRAYS,)),
-        ],
+        in_specs=[SMEM, SMEM] + [ANY if gathered else VMEM] * len(sources) + [ANY] * len(previous),
+        out_specs=(ANY,) * 3,
+        scratch_shapes=scratch,
         input_output_aliases={first + i: i for i in range(len(previous))},
-        compiler_params=pltpu.CompilerParams(vmem_limit_bytes=60 << 20),
+        compiler_params=pltpu.CompilerParams(vmem_limit_bytes=(60 if gathered else 32) << 20),
         cost_estimate=pl.CostEstimate(
-            flops=300 * 2 * 128**3, bytes_accessed=4 << 20, transcendentals=60 * 128 * 128
+            flops=10**6, bytes_accessed=10**4, transcendentals=10**3
         ),
         name="attend",
     )(order, docs, *sources, *previous)
@@ -230,15 +262,14 @@
     blocks = block_order.shape[0]
     devices = lax.axis_size("ctx")
     longest = blocks * 3 // 8
+    arrays = (keys, values, queries, grad_out)
     grads = ()
     if devices != 4:
-        gathered = [
-            lax.all_gather(x, "ctx", axis=0, tiled=True) for x in (queries, keys, values, grad_out)
-        ]
+        whole = [lax.all_gather(x, "ctx", axis=0, tiled=True) for x in arrays]
         for head in range(heads):
-            kernel = functools.partial(attend_gathered, blocks, longest, head)
             grads = attend(
-                kernel, head, gathered, grads, block_order, block_docs, rows, heads, blocks, longest
+                functools.partial(attend_gathered, blocks, longest, head),
+                whole, grads, block_order, block_docs, rows, blocks, longest, heads, True,
             )
         return grads
 
@@ -249,19 +280,29 @@
     own = pl.pallas_call(
         functools.partial(pack_slots, heads),
         out_shape=(slots,) * heads,
-        in_specs=[SMEM] + [VMEM] * ARRAYS,
+        in_specs=[HBM] * (ARRAYS + 1),
         out_specs=(VMEM,) * heads,
-        compiler_params=pltpu.CompilerParams(vmem_limit_bytes=16 << 20),
+        scratch_shapes=[
+            pltpu.SMEM((blocks,), jnp.int32),
+            pltpu.VMEM((ARRAYS, rows, width), jnp.bfloat16),
+            pltpu.SemaphoreType.DMA((ARRAYS + 1,)),
+        ],
+        compiler_params=pltpu.CompilerParams(vmem_limit_bytes=251 << 18),
         name="pack",
-    )(block_order, queries, keys, values, grad_out)
+    )(block_order, *arrays)
     row = [swap(x, 2) for x in own]
     core = [swap(x, 1) for x in own]
-    diag = [swap(x, 1) for x in row]
     for head in range(heads):
-        kernel = functools.partial(attend_slots, blocks, longest)
-        sources = (own[head], core[head], row[head], diag[head])
+        arrived = row[head]
+        if grads:
+            arrived, grads = lax.optimization_barrier((arrived, grads))
+        sources = {(0, 0): own[head], (1, 0): core[head], (2, 0): arrived}
+        pieces = 1 if head == heads - 1 else 4
+        for first in range(0, 4, 4 // pieces):
+            sources[3, first] = swap(arrived[first : first + 4 // pieces], 1)
         grads = attend(
-            kernel, head, sources, grads, block_order, block_docs, rows, heads, blocks, longest
+            functools.partial(attend_slots, blocks, longest, head, tuple(sources)),
+            tuple(sources.values()), grads, block_order, block_docs, rows, blocks, longest, heads, False,
         )
     return grads
 

time: 49.7 us -> 36.5 us (0.73)
  the two profiles are of different devices: /device:TPU:1 before, /device:TPU:19 now
where the time goes in v1:
time: 36.5 us; the launch traced here: 36.4 us
  Pallas kernels  14.3 us (39%)
  waiting for transfers between devices  13.6 us (37%)
  starting transfers between devices  7.74 us (21%)
  between operations  0.67 us (2%)
    ppermute x9, waiting for transfers between devices, swap(): return lax.ppermute(array, 'ctx', [(i, i ^ flip) for i in range(4)])  13.6 us
    pallas_call x2, Pallas kernels, attend(): pl.pallas_call(kernel, out_shape=(out,) * 3, in_specs=[SMEM, SMEM] + [ANY...  11.9 us
    ppermute x9, starting transfers between devices, swap(): return lax.ppermute(array, 'ctx', [(i, i ^ flip) for i in range(4)])  7.74 us
    pallas_call x1, Pallas kernels, local(): pl.pallas_call(functools.partial(pack_slots, heads), out_shape=(slots,) *...  2.44 us
  transfers between devices with their start and end apart: 9, of which 6 were waited for; matrix products, arithmetic and copies ran while one was open for 0% of the time, Pallas kernels for 16%

profile of v1, /device:TPU:19, one launch (start us, length us, event | category | flops | bytes accessed | tf_op | source)
XLA Modules:
  0.0 36.4 jit_solution(7507981350429714309)
XLA Ops:
  0.6 2.4 %pack.1 = (bf16[4,4,128,128]{3,2,1,0:T(8,128)(2,1)}, bf16[4,4,128,128]{3,2,1,0:T(8,128)(2,1)}) custom-call(s32[16]{0:T(128)} %order.3, bf16[512,256]{1,0:T(8,128)(2,1)} %rest_0_.1, bf16[512,256]{1,0:T(8,128)(2,1)} %rest_1_.1, bf16[512,256]{1,0:T(8,128)(2,1)} %rest_2_.1, bf16[512,256]{1,0:T(8,128)(2,1)} %rest_3_.1), custom_call_target="tpu_custom_call" | custom-call | tf_op jit(solution)/shard_map/pack/pallas_call | solution.py:280
  3.1 1.3 %collective-permute-start.3 = (bf16[4,4,128,128]{3,2,1,0:T(8,128)(2,1)}, bf16[4,4,128,128]{3,2,1,0:T(8,128)(2,1)S(1)}, u32[]{:S(2)}, u32[]{:S(2)}) collective-permute-start(bf16[4,4,128,128]{3,2,1,0:T(8,128)(2,1)} %get-tuple-element.13.rest_0_), channel_id=1, source_target_pairs={{0,8},{4,12},{8,0},{12,4},{1,9},{5,13},{9,1},{13,5},{2,10},{6,14},... | collective-permute-start | bytes 1572872 | tf_op jit(solution)/shard_map/ppermute | solution.py:277
  4.4 1.0 %collective-permute-start.2 = (bf16[4,4,128,128]{3,2,1,0:T(8,128)(2,1)}, bf16[4,4,128,128]{3,2,1,0:T(8,128)(2,1)S(1)}, u32[]{:S(2)}, u32[]{:S(2)}) collective-permute-start(bf16[4,4,128,128]{3,2,1,0:T(8,128)(2,1)} %get-tuple-element.13.rest_0_), channel_id=1, source_target_pairs={{0,4},{4,0},{8,12},{12,8},{1,5},{5,1},{9,13},{13,9},{2,6},{6,2},{1... | collective-permute-start | bytes 1572872 | tf_op jit(solution)/shard_map/ppermute | solution.py:277
  5.3 0.0 copy-start
  5.3 0.0 copy-start.1
  5.3 0.2 collective-permute-start.1
  5.6 10.6 %collective-permute-done.3.rest_2_ = bf16[4,4,128,128]{3,2,1,0:T(8,128)(2,1)S(1)} collective-permute-done((bf16[4,4,128,128]{3,2,1,0:T(8,128)(2,1)}, bf16[4,4,128,128]{3,2,1,0:T(8,128)(2,1)S(1)}, u32[]{:S(2)}, u32[]{:S(2)}) %collective-permute-start.3) | collective-permute-done | bytes 524320 | tf_op jit(solution)/shard_map/ppermute | solution.py:277
  16.2 2.8 %collective-permute-start.4 = (bf16[1,4,128,128]{3,2,1,0:T(8,128)(2,1)S(1)}, bf16[1,4,128,128]{3,2,1,0:T(8,128)(2,1)S(1)}, u32[]{:S(2)}, u32[]{:S(2)}) collective-permute-start(bf16[1,4,128,128]{3,2,1,0:T(8,128)(2,1)S(1)} %get-tuple-element.24), channel_id=1, source_target_pairs={{0,4},{4,0},{8,12},{12,8},{1,5},{5,1},{9,13},{13,9},{2,6},{6,2},{1... | collective-permute-start | bytes 393224 | tf_op jit(solution)/shard_map/ppermute | solution.py:277
  18.9 0.1 collective-permute-start.5
  19.0 0.0 copy-start.2
  19.0 0.0 copy-start.3
  19.0 0.4 %collective-permute-start.6 = (bf16[1,4,128,128]{3,2,1,0:T(8,128)(2,1)S(1)}, bf16[1,4,128,128]{3,2,1,0:T(8,128)(2,1)S(1)}, u32[]{:S(2)}, u32[]{:S(2)}) collective-permute-start(bf16[1,4,128,128]{3,2,1,0:T(8,128)(2,1)S(1)} %get-tuple-element.22), channel_id=1, source_target_pairs={{0,4},{4,0},{8,12},{12,8},{1,5},{5,1},{9,13},{13,9},{2,6},{6,2},{1... | collective-permute-start | bytes 393224 | tf_op jit(solution)/shard_map/ppermute | solution.py:277
  19.5 0.0 collective-permute-done.2.rest_1_
  19.5 0.1 collective-permute-start.7
  19.5 0.4 %collective-permute-done.4.rest_3_ = bf16[1,4,128,128]{3,2,1,0:T(8,128)(2,1)S(1)} collective-permute-done((bf16[1,4,128,128]{3,2,1,0:T(8,128)(2,1)S(1)}, bf16[1,4,128,128]{3,2,1,0:T(8,128)(2,1)S(1)}, u32[]{:S(2)}, u32[]{:S(2)}) %collective-permute-start.4) | collective-permute-done | bytes 131104 | tf_op jit(solution)/shard_map/ppermute | solution.py:277
  19.9 0.0 copy-done
  19.9 0.4 collective-permute-start
  20.3 0.0 collective-permute-done.5.rest_4_
  20.3 0.2 collective-permute-done.6.rest_5_
  20.5 0.3 collective-permute-done.7.rest_6_
  20.8 0.0 copy-done.1
  20.8 0.0 copy-done.2
  20.8 0.0 copy-done.3
  20.8 6.0 %attend.2 = (bf16[512,256]{1,0:T(8,128)(2,1)}, bf16[512,256]{1,0:T(8,128)(2,1)}, bf16[512,256]{1,0:T(8,128)(2,1)}) custom-call(s32[16]{0:T(128)S(1)} %copy-done.2, s32[16]{0:T(128)S(1)} %copy-done.3, bf16[4,4,128,128]{3,2,1,0:T(8,128)(2,1)S(1)} %copy-done.1, bf16[4,4,128,128]{3,2,1,0:T(8,128)(2,1)S(1)} %collective-permute-done.2.rest_1_, ...), custom_call_target="tpu_custom_call" | custom-call | flops 1000000 | bytes 10000 | tf_op jit(solution)/shard_map/attend/pallas_call | solution.py:244
  26.8 0.6 %collective-permute-done.1.rest_2_ = bf16[4,4,128,128]{3,2,1,0:T(8,128)(2,1)S(1)} collective-permute-done((bf16[4,4,128,128]{3,2,1,0:T(8,128)(2,1)}, bf16[4,4,128,128]{3,2,1,0:T(8,128)(2,1)S(1)}, u32[]{:S(2)}, u32[]{:S(2)}) %collective-permute-start.1) | collective-permute-done | bytes 524320 | tf_op jit(solution)/shard_map/ppermute | solution.py:277
  27.4 1.5 %collective-permute-start.8 = (bf16[4,4,128,128]{3,2,1,0:T(8,128)(2,1)S(1)}, bf16[4,4,128,128]{3,2,1,0:T(8,128)(2,1)S(1)}, u32[]{:S(2)}, u32[]{:S(2)}) collective-permute-start(bf16[4,4,128,128]{3,2,1,0:T(8,128)(2,1)S(1)} %collective-permute-done.1.rest_2_), channel_id=1, source_target_pairs={{0,4},{4,0},{8,12},{12,8},{1,5},{5,1},{9,13},{13,9},{2,6},{6,2},{1... | collective-permute-start | bytes 1572872 | tf_op jit(solution)/shard_map/ppermute | solution.py:277
  28.9 0.0 collective-permute-done.rest_1_
  28.9 1.5 %collective-permute-done.8.rest_3_ = bf16[4,4,128,128]{3,2,1,0:T(8,128)(2,1)S(1)} collective-permute-done((bf16[4,4,128,128]{3,2,1,0:T(8,128)(2,1)S(1)}, bf16[4,4,128,128]{3,2,1,0:T(8,128)(2,1)S(1)}, u32[]{:S(2)}, u32[]{:S(2)}) %collective-permute-start.8) | collective-permute-done | bytes 524320 | tf_op jit(solution)/shard_map/ppermute | solution.py:277
  30.5 6.0 %attend.3 = (bf16[512,256]{1,0:T(8,128)(2,1)}, bf16[512,256]{1,0:T(8,128)(2,1)}, bf16[512,256]{1,0:T(8,128)(2,1)}) custom-call(s32[16]{0:T(128)S(1)} %copy-done.2, s32[16]{0:T(128)S(1)} %copy-done.3, bf16[4,4,128,128]{3,2,1,0:T(8,128)(2,1)S(1)} %copy-done, ...), custom_call_target="tpu_custom_call", output_to_operand_aliasing={{0}: (6, {}), {1}: (7, {}), {2}: (8, {})} | custom-call | flops 1000000 | bytes 10000 | tf_op jit(solution)/shard_map/attend/pallas_call | solution.py:244
  (1 shorter events, 0.0 us)
Async XLA Ops:
  3.1 13.1 %collective-permute-start.3 = (bf16[4,4,128,128]{3,2,1,0:T(8,128)(2,1)}, bf16[4,4,128,128]{3,2,1,0:T(8,128)(2,1)S(1)}, u32[]{:S(2)}, u32[]{:S(2)}) collective-permute-start(bf16[4,4,128,128]{3,2,1,0:T(8,128)(2,1)} %get-tuple-element.13.rest_0_), channel_id=1, source_target_pairs={{0,8},{4,12},{8,0},{12,4},{1,9},{5,13},{9,1},{13,5},{2,10},{6,14},... | collective-permute-start | bytes 1572872 | tf_op jit(solution)/shard_map/ppermute | solution.py:277
  4.4 15.1 %collective-permute-start.2 = (bf16[4,4,128,128]{3,2,1,0:T(8,128)(2,1)}, bf16[4,4,128,128]{3,2,1,0:T(8,128)(2,1)S(1)}, u32[]{:S(2)}, u32[]{:S(2)}) collective-permute-start(bf16[4,4,128,128]{3,2,1,0:T(8,128)(2,1)} %get-tuple-element.13.rest_0_), channel_id=1, source_target_pairs={{0,4},{4,0},{8,12},{12,8},{1,5},{5,1},{9,13},{13,9},{2,6},{6,2},{1... | collective-permute-start | bytes 1572872 | tf_op jit(solution)/shard_map/ppermute | solution.py:277
  5.3 14.6 %copy-start = (bf16[4,4,128,128]{3,2,1,0:T(8,128)(2,1)S(1)}, bf16[4,4,128,128]{3,2,1,0:T(8,128)(2,1)}, u32[]{:S(2)}) copy-start(bf16[4,4,128,128]{3,2,1,0:T(8,128)(2,1)} %get-tuple-element.12.rest_0_) | copy-start | bytes 1572868
  5.3 15.5 %copy-start.1 = (bf16[4,4,128,128]{3,2,1,0:T(8,128)(2,1)S(1)}, bf16[4,4,128,128]{3,2,1,0:T(8,128)(2,1)}, u32[]{:S(2)}) copy-start(bf16[4,4,128,128]{3,2,1,0:T(8,128)(2,1)} %get-tuple-element.13.rest_0_) | copy-start | bytes 1572868
  5.3 22.0 %collective-permute-start.1 = (bf16[4,4,128,128]{3,2,1,0:T(8,128)(2,1)}, bf16[4,4,128,128]{3,2,1,0:T(8,128)(2,1)S(1)}, u32[]{:S(2)}, u32[]{:S(2)}) collective-permute-start(bf16[4,4,128,128]{3,2,1,0:T(8,128)(2,1)} %get-tuple-element.12.rest_0_), channel_id=1, source_target_pairs={{0,8},{4,12},{8,0},{12,4},{1,9},{5,13},{9,1},{13,5},{2,10},{6,14},... | collective-permute-start | bytes 1572872 | tf_op jit(solution)/shard_map/ppermute | solution.py:277
  16.2 3.7 %collective-permute-start.4 = (bf16[1,4,128,128]{3,2,1,0:T(8,128)(2,1)S(1)}, bf16[1,4,128,128]{3,2,1,0:T(8,128)(2,1)S(1)}, u32[]{:S(2)}, u32[]{:S(2)}) collective-permute-start(bf16[1,4,128,128]{3,2,1,0:T(8,128)(2,1)S(1)} %get-tuple-element.24), channel_id=1, source_target_pairs={{0,4},{4,0},{8,12},{12,8},{1,5},{5,1},{9,13},{13,9},{2,6},{6,2},{1... | collective-permute-start | bytes 393224 | tf_op jit(solution)/shard_map/ppermute | solution.py:277
  18.9 1.4 %collective-permute-start.5 = (bf16[1,4,128,128]{3,2,1,0:T(8,128)(2,1)S(1)}, bf16[1,4,128,128]{3,2,1,0:T(8,128)(2,1)S(1)}, u32[]{:S(2)}, u32[]{:S(2)}) collective-permute-start(bf16[1,4,128,128]{3,2,1,0:T(8,128)(2,1)S(1)} %get-tuple-element.23), channel_id=1, source_target_pairs={{0,4},{4,0},{8,12},{12,8},{1,5},{5,1},{9,13},{13,9},{2,6},{6,2},{1... | collective-permute-start | bytes 393224 | tf_op jit(solution)/shard_map/ppermute | solution.py:277
  19.0 1.8 %copy-start.2 = (s32[16]{0:T(128)S(1)}, s32[16]{0:T(128)}, u32[]{:S(2)}) copy-start(s32[16]{0:T(128)} %order.3) | copy-start | bytes 196
  19.0 1.8 %copy-start.3 = (s32[16]{0:T(128)S(1)}, s32[16]{0:T(128)}, u32[]{:S(2)}) copy-start(s32[16]{0:T(128)} %docs.3) | copy-start | bytes 196
  19.0 1.5 %collective-permute-start.6 = (bf16[1,4,128,128]{3,2,1,0:T(8,128)(2,1)S(1)}, bf16[1,4,128,128]{3,2,1,0:T(8,128)(2,1)S(1)}, u32[]{:S(2)}, u32[]{:S(2)}) collective-permute-start(bf16[1,4,128,128]{3,2,1,0:T(8,128)(2,1)S(1)} %get-tuple-element.22), channel_id=1, source_target_pairs={{0,4},{4,0},{8,12},{12,8},{1,5},{5,1},{9,13},{13,9},{2,6},{6,2},{1... | collective-permute-start | bytes 393224 | tf_op jit(solution)/shard_map/ppermute | solution.py:277
  19.5 1.3 %collective-permute-start.7 = (bf16[1,4,128,128]{3,2,1,0:T(8,128)(2,1)S(1)}, bf16[1,4,128,128]{3,2,1,0:T(8,128)(2,1)S(1)}, u32[]{:S(2)}, u32[]{:S(2)}) collective-permute-start(bf16[1,4,128,128]{3,2,1,0:T(8,128)(2,1)S(1)} %get-tuple-element.21), channel_id=1, source_target_pairs={{0,4},{4,0},{8,12},{12,8},{1,5},{5,1},{9,13},{13,9},{2,6},{6,2},{1... | collective-permute-start | bytes 393224 | tf_op jit(solution)/shard_map/ppermute | solution.py:277
  19.9 9.0 %collective-permute-start = (bf16[4,4,128,128]{3,2,1,0:T(8,128)(2,1)S(1)}, bf16[4,4,128,128]{3,2,1,0:T(8,128)(2,1)S(1)}, u32[]{:S(2)}, u32[]{:S(2)}) collective-permute-start(bf16[4,4,128,128]{3,2,1,0:T(8,128)(2,1)S(1)} %copy-done), channel_id=1, source_target_pairs={{0,4},{4,0},{8,12},{12,8},{1,5},{5,1},{9,13},{13,9},{2,6},{6,2},{1... | collective-permute-start | bytes 1572872 | tf_op jit(solution)/shard_map/ppermute | solution.py:277
  27.4 3.1 %collective-permute-start.8 = (bf16[4,4,128,128]{3,2,1,0:T(8,128)(2,1)S(1)}, bf16[4,4,128,128]{3,2,1,0:T(8,128)(2,1)S(1)}, u32[]{:S(2)}, u32[]{:S(2)}) collective-permute-start(bf16[4,4,128,128]{3,2,1,0:T(8,128)(2,1)S(1)} %collective-permute-done.1.rest_2_), channel_id=1, source_target_pairs={{0,4},{4,0},{8,12},{12,8},{1,5},{5,1},{9,13},{13,9},{2,6},{6,2},{1... | collective-permute-start | bytes 1572872 | tf_op jit(solution)/shard_map/ppermute | solution.py:277
